TPU v7x, 512 devices: a whole 4x4x16 slice. The times are simulated.
512 devices in a mesh: snd: 32 (over z, core), freq: 4 (over x), mesh: 4 (over y).
Axes of the slice: x: 4, y: 4, z: 16, core: 2. Of those that a mesh axis runs over, the one named last changes fastest.
Arguments:
- source: float32 [32, 6, 32, 3072], P('snd', None, 'mesh'), may hold values from -6 to 6
- adjoint: float32 [32, 4, 6, 32, 3072], P('snd', 'freq', None, 'mesh'), may hold values from -3 to 3
- omegas: float32 [4], P('freq'), may hold values from 0.5 to 8
- background: float32 [3], replicated, may hold values from 0.1 to 1
- conductivity: float32 [8192, 384], P(('snd', 'mesh')), may hold values from 0.05 to 5
- block_owner: int32 [32, 768, 1], P('snd', 'mesh'), may hold values from 0 to 127; in each aligned block of 192 rows (0 to 191, 192 to 383, ..., all dimensions but the last counted through in order) at most 4 rows name the same one
- block_local: int32 [32, 768], P('snd', 'mesh'), may hold values from 0 to 63
- block_count: int32 [32], P('snd'), may hold values from 384 to 768
Outputs:
- field: float32 [32, 4, 6, 32, 3072], P('snd', 'freq', None, 'mesh')
- gradient: float32 [8192, 384], P(('snd', 'mesh'))
Inputs may be any that keep to these rules, and one draw needn't show every extreme that they name: `block_owner`: among the 192 blocks of one device (aligned blocks of rows of one footprint) no owner appears more than 4 times, and some owner appears exactly 4 times in some device's blocks.
All inputs are finite; a program needn't handle non-finite values.
Results may differ from a plain program's by a relative error of at most 0.0003.
Values sent between devices are 32-bit elements; how exact they have to be, the bound alone decides.
A program may use at most 64 MiB of HBM per device.

v0:
```python
import jax
import jax.numpy as jnp
from jax import lax
from jax.sharding import PartitionSpec as P

NY = 64
NZ = 48
ITERS = 4


RELAX_FACTOR = 0.5


def with_halo(x, sides, width):
    for axis, dim in sides:
        peers, length = (lax.axis_size(axis), x.shape[dim])
        up = [(i, (i + 1) % peers) for i in range(peers - 1)]
        down = [(j, i) for i, j in up]
        last = lax.slice_in_dim(x, length - width, length, axis=dim)
        leading = lax.slice_in_dim(x, 0, width, axis=dim)
        before = lax.ppermute(last, axis, up)
        after = lax.ppermute(leading, axis, down)
        x = jnp.concatenate([before, x, after], axis=dim)
    return x


def ahead_cells(values, offset, keep):
    padded = jnp.pad(values, [(0, 0)] * (values.ndim - 1) + [(0, offset)])
    return padded[..., offset:] * keep


def behind_cells(values, offset, keep):
    padded = jnp.pad(values, [(0, 0)] * (values.ndim - 1) + [(offset, 0)])
    return padded[..., :-offset] * keep


def cell_masks(count_second, count_third):
    cell_index = jnp.arange(count_second * count_third, dtype=jnp.int32)
    third_coord = cell_index % count_third
    second_coord = cell_index // count_third
    third_up = (third_coord < count_third - 1).astype(jnp.float32)
    third_down = (third_coord > 0).astype(jnp.float32)
    second_up = (second_coord < count_second - 1).astype(jnp.float32)
    second_down = (second_coord > 0).astype(jnp.float32)
    return (third_up, third_down, second_up, second_down)


def curl_curl(padded_field, keep_first, edge_masks, count_third):
    third_up, third_down, second_up, second_down = edge_masks
    components = padded_field.reshape(2, 3, padded_field.shape[1], padded_field.shape[2])
    along_first = components[:, 0]
    along_second = components[:, 1]
    along_third = components[:, 2]

    def step_first(values):
        return values[:, 1:] - values[:, :-1]

    def step_second(values):
        return ahead_cells(values[:, :-1], count_third, second_up) - values[:, :-1]

    def step_third(values):
        return ahead_cells(values[:, :-1], 1, third_up) - values[:, :-1]

    curl_first = step_second(along_third) - step_third(along_second)
    curl_second = step_third(along_first) - step_first(along_third)
    curl_third = step_first(along_second) - step_second(along_first)
    row_count = curl_first.shape[1]
    first_row = (jnp.arange(row_count) == 0)[None, :, None]
    row_scale = jnp.where(first_row, keep_first, 1.0)
    curl_first = curl_first * row_scale
    curl_second = curl_second * row_scale
    curl_third = curl_third * row_scale

    def back_first(values):
        return values[:, :-1] - values[:, 1:]

    def back_second(values):
        return behind_cells(values[:, 1:], count_third, second_down) - values[:, 1:]

    def back_third(values):
        return behind_cells(values[:, 1:], 1, third_down) - values[:, 1:]

    image_first = back_third(curl_second) - back_second(curl_third)
    image_second = back_first(curl_third) - back_third(curl_first)
    image_third = back_second(curl_first) - back_first(curl_second)
    return jnp.stack([image_first, image_second, image_third], axis=1)


def relax_step(field_now, forcing, applied, weights):
    field_real = field_now[:3]
    field_imag = field_now[3:]
    resid_real = forcing[:3] - applied[:3] + weights * field_imag
    resid_imag = forcing[3:] - applied[3:] - weights * field_real
    denominator = 16.0 + weights * weights
    new_real = field_real + RELAX_FACTOR * (4.0 * resid_real + weights * resid_imag) / denominator
    new_imag = field_imag + RELAX_FACTOR * (4.0 * resid_imag - weights * resid_real) / denominator
    return jnp.concatenate([new_real, new_imag], axis=0)


def on_device(
    source, adjoint, omegas, background, conductivity, block_owner, block_local, block_count
):
    snd_count = lax.axis_size("snd")
    mesh_count = lax.axis_size("mesh")
    freq_count = lax.axis_size("freq")
    owner_total = snd_count * mesh_count
    block_total = block_local.shape[1]
    capacity = freq_count * (
        (block_total * 5 // 4 + freq_count * owner_total - 1) // (freq_count * owner_total)
    )
    block_first = lax.axis_index("mesh") * block_total
    live_flags = block_first + jnp.arange(block_total, dtype=jnp.int32) < block_count[0]
    owner_index = block_owner[0, :, 0]
    local_index = block_local[0]
    owner_table = (
        (owner_index[:, None] == jnp.arange(owner_total, dtype=jnp.int32)[None, :])
        & live_flags[:, None]
    ).astype(jnp.int32)
    slot_rank = jnp.sum((jnp.cumsum(owner_table, axis=0) - 1) * owner_table, axis=1)
    slot_place = jnp.where(live_flags, owner_index * capacity + slot_rank, owner_total * capacity)
    requests = (
        jnp.full((owner_total * capacity,), -1, jnp.int32)
        .at[slot_place]
        .set(local_index, mode="drop")
    )
    requests = requests.reshape(owner_total, capacity)
    arrived = lax.all_to_all(requests, ("snd", "mesh"), split_axis=0, concat_axis=0, tiled=True)
    looked = jnp.take(conductivity, jnp.maximum(arrived, 0), axis=0)
    looked = jnp.where((arrived >= 0)[:, :, None], looked, 0.0)
    replies = lax.all_to_all(looked, ("snd", "mesh"), split_axis=0, concat_axis=0, tiled=True)
    fetched_rows = replies.reshape(owner_total * capacity, 384)
    picked = jnp.take(fetched_rows, jnp.minimum(slot_place, owner_total * capacity - 1), axis=0)
    base_row = jnp.repeat(background, 128)
    sigma_blocks = jnp.where(live_flags[:, None], picked, base_row[None, :])
    rows_local = source.shape[2]
    plane_cells = source.shape[3]
    sigma_field = (
        sigma_blocks.reshape(block_total, 3, 128)
        .transpose(1, 0, 2)
        .reshape(3, rows_local, plane_cells)
    )
    weights = omegas[0] * sigma_field
    forcing = source[0]
    adjoint_field = adjoint[0, 0]
    edge_masks = cell_masks(NY, NZ)
    keep_first = (lax.axis_index("mesh") > 0).astype(jnp.float32)
    field_now = jnp.zeros_like(forcing)
    for step_index in range(ITERS):
        if step_index == 0:
            applied = jnp.zeros_like(forcing)
        else:
            padded = with_halo(field_now, (("mesh", 1),), 1)
            applied = curl_curl(padded, keep_first, edge_masks, NZ).reshape(
                6, rows_local, plane_cells
            )
        field_now = relax_step(field_now, forcing, applied, weights)
    sensitivity = omegas[0] * (
        adjoint_field[:3] * field_now[3:] - adjoint_field[3:] * field_now[:3]
    )
    grad_blocks = (
        sensitivity.reshape(3, block_total, 128).transpose(1, 0, 2).reshape(block_total, 384)
    )
    grad_slots = (
        jnp.zeros((owner_total * capacity, 384), jnp.float32)
        .at[slot_place]
        .set(grad_blocks, mode="drop")
    )
    grad_slots = grad_slots.reshape(owner_total, capacity, 384)
    received = lax.all_to_all(grad_slots, ("snd", "mesh"), split_axis=0, concat_axis=0, tiled=True)
    slot_ids = arrived.reshape(-1)
    owner_onehot = (
        jnp.arange(conductivity.shape[0], dtype=jnp.int32)[:, None] == slot_ids[None, :]
    ).astype(jnp.float32)
    partial_value = jnp.dot(
        owner_onehot,
        received.reshape(-1, 384),
        precision=lax.Precision.HIGHEST,
        preferred_element_type=jnp.float32,
    )
    gradient = lax.psum(partial_value, "freq")
    return (field_now[None, None], gradient)


def solution(mesh):
    return jax.shard_map(
        on_device,
        mesh=mesh,
        in_specs=(
            P("snd", None, "mesh", None),
            P("snd", "freq", None, "mesh", None),
            P("freq"),
            P(),
            P(("snd", "mesh"), None),
            P("snd", "mesh", None),
            P("snd", "mesh"),
            P("snd"),
        ),
        out_specs=(P("snd", "freq", None, "mesh", None), P(("snd", "mesh"), None)),
        check_vma=False,
    )
```

profile of v0, /device:TPU:1, one launch (start us, length us, event | category | flops | bytes accessed | tf_op | source)
XLA Modules:
  0.0 256.9 jit_solution(2095587871946302486)
XLA Ops:
  8.9 0.9 fusion.90
  10.5 1.4 scatter_custom_fusion
  12.0 36.1 %all_to_all.19 = s32[128,1,4]{2,1,0:T(1,128)S(1)} all-to-all(s32[128,1,4]{2,1,0:T(1,128)S(1)} %bitcast.255), channel_id=1, replica_groups=mesh['snd'=32,'freq'=4,'mesh'=4] {'snd','mesh'}, dimensions={0} | all-to-all | bytes 4096 | tf_op jit(solution)/shard_map/all_to_all | solution.py:127
  48.7 1.6 gather_fusion
  50.5 1.3 select_select_fusion
  51.8 5.5 %all-to-all-start.1 = ((f32[128,4,384]{2,1,0:T(4,128)}), f32[128,4,384]{2,1,0:T(4,128)S(1)}, u32[]{:S(2)}, u32[]{:S(2)}) async-start(f32[128,4,384]{2,1,0:T(4,128)} %select_select_fusion), calls=%async_computation.1 | async-start | bytes 1572864 | tf_op jit(solution)/shard_map/all_to_all | solution.py:130
  59.4 42.4 %all-to-all-done.1 = f32[128,4,384]{2,1,0:T(4,128)S(1)} async-done(((f32[128,4,384]{2,1,0:T(4,128)}), f32[128,4,384]{2,1,0:T(4,128)S(1)}, u32[]{:S(2)}, u32[]{:S(2)}) %all-to-all-start.1) | async-done | bytes 786464 | tf_op jit(solution)/shard_map/all_to_all | solution.py:130
  102.1 0.9 gather_fusion.1
  103.4 3.1 %collective-permute-start = (f32[6,1,3072]{2,1,0:T(1,128)S(1)}, f32[6,1,3072]{2,1,0:T(1,128)S(1)}, u32[]{:S(2)}, u32[]{:S(2)}) collective-permute-start(f32[6,1,3072]{2,1,0:T(1,128)S(1)} %get-tuple-element.35), channel_id=1, source_target_pairs={{0,1},{1,2},{2,3},{4,5},{5,6},{6,7},{8,9},{9,10},{10,11},{12,13},{... | collective-permute-start | bytes 221192 | tf_op jit(solution)/shard_map/ppermute | solution.py:21
  106.5 1.3 collective-permute-start.1
  107.9 3.7 %collective-permute-done.1 = f32[6,1,3072]{2,1,0:T(1,128)S(1)} collective-permute-done((f32[6,1,3072]{2,1,0:T(1,128)S(1)}, f32[6,1,3072]{2,1,0:T(1,128)S(1)}, u32[]{:S(2)}, u32[]{:S(2)}) %collective-permute-start.1) | collective-permute-done | bytes 73760 | tf_op jit(solution)/shard_map/ppermute | solution.py:22
  114.1 4.4 %collective-permute-start.2 = (f32[6,1,3072]{2,1,0:T(1,128)}, f32[6,1,3072]{2,1,0:T(1,128)}, u32[]{:S(2)}, u32[]{:S(2)}) collective-permute-start(f32[6,1,3072]{2,1,0:T(1,128)} %get-tuple-element.33), channel_id=1, source_target_pairs={{0,1},{1,2},{2,3},{4,5},{5,6},{6,7},{8,9},{9,10},{10,11},{12,13},{... | collective-permute-start | bytes 221192 | tf_op jit(solution)/shard_map/ppermute | solution.py:21
  118.5 1.3 collective-permute-start.3
  121.4 2.3 collective-permute-done.3
  123.7 1.1 pad_maximum_fusion.1
  127.1 2.5 collective-permute-start.4
  129.6 1.3 collective-permute-start.5
  132.5 2.3 collective-permute-done.5
  134.8 1.1 pad_maximum_fusion.2
  137.3 0.8 fusion.107
  138.1 1.7 slice.436
  139.8 1.7 slice.437
  141.6 3.1 %multiply_bitcast_fusion = f32[3,24,8,128]{3,2,1,0:T(8,128)} fusion(f32[3,192,128]{2,1,0:T(8,128)} %slice.439, f32[3,192,128]{2,1,0:T(8,128)S(1)} %slice.429, f32[3,192,128]{2,1,0:T(8,128)S(1)} %slice.431, f32[3,192,128]{2,1,0:T(8,128)} %slice.437, f32[3,192,128]{2,1,0:T(8,128)S(1)} %slice.430, f32[3,192,128]{2,1,0:T(8,128)} %slice.436, ...), kind=kLoop, calls=%fused_computation.85 | loop fusion | flops 5603328 | bytes 3539344
  144.6 1.9 scatter_custom_fusion.1
  146.5 1.1 reshape.234
  147.6 9.0 %all-to-all-start.2 = ((f32[128,4,384]{2,1,0:T(4,128)}), f32[128,4,384]{2,1,0:T(4,128)S(1)}, u32[]{:S(2)}, u32[]{:S(2)}) async-start(f32[128,4,384]{2,1,0:T(4,128)} %reshape.234), calls=%async_computation.2 | async-start | bytes 1572864 | tf_op jit(solution)/shard_map/all_to_all | solution.py:169
  158.1 1.0 divide_add_fusion.1
  159.2 42.0 %all-to-all-done.2 = f32[128,4,384]{2,1,0:T(4,128)S(1)} async-done(((f32[128,4,384]{2,1,0:T(4,128)}), f32[128,4,384]{2,1,0:T(4,128)S(1)}, u32[]{:S(2)}, u32[]{:S(2)}) %all-to-all-start.2) | async-done | bytes 786464 | tf_op jit(solution)/shard_map/all_to_all | solution.py:169
  201.4 1.1 fusion.88
  202.6 0.9 maximum_bitcast_fusion
  203.4 45.1 %all-reduce.27.cloned.1.call-done = f32[64,384]{1,0:T(8,128)} async-done(((f32[64,384]{1,0:T(8,128)}), f32[64,384]{1,0:T(8,128)}) %all-reduce.27.cloned.1.call-update) | async-done | bytes 98320 | tf_op jit(solution)/shard_map/psum | solution.py:180
  248.5 1.5 copy.247
  (100 shorter events, 15.6 us)
Async XLA Ops:
  7.2 41.5 %copy-start = (f32[64,384]{1,0:T(8,128)S(1)}, f32[64,384]{1,0:T(8,128)}, u32[]{:S(2)}) copy-start(f32[64,384]{1,0:T(8,128)} %param.12) | copy-start | bytes 294916
  51.8 6.3 %copy-start.4 = (f32[1,1,6,8,3072]{4,3,2,1,0:T(8,128)S(1)}, f32[1,1,6,8,3072]{4,3,2,1,0:T(8,128)}, u32[]{:S(2)}) copy-start(f32[1,1,6,8,3072]{4,3,2,1,0:T(8,128)} %param.9) | copy-start | bytes 1769476
  51.8 50.0 %all-to-all-start.1 = ((f32[128,4,384]{2,1,0:T(4,128)}), f32[128,4,384]{2,1,0:T(4,128)S(1)}, u32[]{:S(2)}, u32[]{:S(2)}) async-start(f32[128,4,384]{2,1,0:T(4,128)} %select_select_fusion), calls=%async_computation.1 | async-start | bytes 1572864 | tf_op jit(solution)/shard_map/all_to_all | solution.py:130
  57.3 1.1 copy-start.1
  58.4 0.9 copy-start.5
  102.1 0.9 copy-start.6
  103.4 4.5 %collective-permute-start = (f32[6,1,3072]{2,1,0:T(1,128)S(1)}, f32[6,1,3072]{2,1,0:T(1,128)S(1)}, u32[]{:S(2)}, u32[]{:S(2)}) collective-permute-start(f32[6,1,3072]{2,1,0:T(1,128)S(1)} %get-tuple-element.35), channel_id=1, source_target_pairs={{0,1},{1,2},{2,3},{4,5},{5,6},{6,7},{8,9},{9,10},{10,11},{12,13},{... | collective-permute-start | bytes 221192 | tf_op jit(solution)/shard_map/ppermute | solution.py:21
  106.5 5.1 %collective-permute-start.1 = (f32[6,1,3072]{2,1,0:T(1,128)S(1)}, f32[6,1,3072]{2,1,0:T(1,128)S(1)}, u32[]{:S(2)}, u32[]{:S(2)}) collective-permute-start(f32[6,1,3072]{2,1,0:T(1,128)S(1)} %get-tuple-element.36), channel_id=1, source_target_pairs={{1,0},{2,1},{3,2},{5,4},{6,5},{7,6},{9,8},{10,9},{11,10},{13,12},{... | collective-permute-start | bytes 221192 | tf_op jit(solution)/shard_map/ppermute | solution.py:22
  114.1 7.3 %collective-permute-start.2 = (f32[6,1,3072]{2,1,0:T(1,128)}, f32[6,1,3072]{2,1,0:T(1,128)}, u32[]{:S(2)}, u32[]{:S(2)}) collective-permute-start(f32[6,1,3072]{2,1,0:T(1,128)} %get-tuple-element.33), channel_id=1, source_target_pairs={{0,1},{1,2},{2,3},{4,5},{5,6},{6,7},{8,9},{9,10},{10,11},{12,13},{... | collective-permute-start | bytes 221192 | tf_op jit(solution)/shard_map/ppermute | solution.py:21
  118.5 5.2 %collective-permute-start.3 = (f32[6,1,3072]{2,1,0:T(1,128)S(1)}, f32[6,1,3072]{2,1,0:T(1,128)}, u32[]{:S(2)}, u32[]{:S(2)}) collective-permute-start(f32[6,1,3072]{2,1,0:T(1,128)S(1)} %get-tuple-element.34), channel_id=1, source_target_pairs={{1,0},{2,1},{3,2},{5,4},{6,5},{7,6},{9,8},{10,9},{11,10},{13,12},{... | collective-permute-start | bytes 221192 | tf_op jit(solution)/shard_map/ppermute | solution.py:22
  127.1 5.4 %collective-permute-start.4 = (f32[6,1,3072]{2,1,0:T(1,128)}, f32[6,1,3072]{2,1,0:T(1,128)}, u32[]{:S(2)}, u32[]{:S(2)}) collective-permute-start(f32[6,1,3072]{2,1,0:T(1,128)} %get-tuple-element.31), channel_id=1, source_target_pairs={{0,1},{1,2},{2,3},{4,5},{5,6},{6,7},{8,9},{9,10},{10,11},{12,13},{... | collective-permute-start | bytes 221192 | tf_op jit(solution)/shard_map/ppermute | solution.py:21
  129.6 5.2 %collective-permute-start.5 = (f32[6,1,3072]{2,1,0:T(1,128)S(1)}, f32[6,1,3072]{2,1,0:T(1,128)}, u32[]{:S(2)}, u32[]{:S(2)}) collective-permute-start(f32[6,1,3072]{2,1,0:T(1,128)S(1)} %get-tuple-element.32), channel_id=1, source_target_pairs={{1,0},{2,1},{3,2},{5,4},{6,5},{7,6},{9,8},{10,9},{11,10},{13,12},{... | collective-permute-start | bytes 221192 | tf_op jit(solution)/shard_map/ppermute | solution.py:22
  147.6 53.5 %all-to-all-start.2 = ((f32[128,4,384]{2,1,0:T(4,128)}), f32[128,4,384]{2,1,0:T(4,128)S(1)}, u32[]{:S(2)}, u32[]{:S(2)}) async-start(f32[128,4,384]{2,1,0:T(4,128)} %reshape.234), calls=%async_computation.2 | async-start | bytes 1572864 | tf_op jit(solution)/shard_map/all_to_all | solution.py:169
  156.7 91.8 %all-reduce.27.cloned.1.call-start = ((), (), s32[]{:S(2)}) async-start(), calls=%async_computation.3 | async-start | bytes 196608 | tf_op jit(solution)/shard_map/psum | solution.py:180
  159.2 43.3 %copy-start.2 = (f32[3,8,3072]{2,1,0:T(8,128)S(1)}, f32[3,8,3072]{2,1,0:T(8,128)}, u32[]{:S(2)}) copy-start(f32[3,8,3072]{2,1,0:T(8,128)} %get-tuple-element.4) | copy-start | bytes 884740
  159.2 43.4 %copy-start.3 = (f32[3,8,3072]{2,1,0:T(8,128)S(1)}, f32[3,8,3072]{2,1,0:T(8,128)}, u32[]{:S(2)}) copy-start(f32[3,8,3072]{2,1,0:T(8,128)} %get-tuple-element.5) | copy-start | bytes 884740
Sparse Core Ops, SparseCore 0:
  202.7 45.7 all-reduce.26
where the time goes:
time: 259 us; the launch traced here: 257 us
  waiting for transfers between devices  138 us (53%)
  blocking collectives  36.1 us (14%)
  starting transfers between devices  28.4 us (11%)
  local copies, waits for them, and re-layouts  20.3 us (8%)
  other arithmetic  17.1 us (7%)
  between operations  16 us (6%)
    psum x1, waiting for transfers between devices, on_device(): gradient = lax.psum(partial_value, 'freq')  45.1 us
    all_to_all x1, waiting for transfers between devices, on_device(): lax.all_to_all(looked, ('snd', 'mesh'), split_axis=0, concat_axis=0, tile...  42.4 us
    all_to_all x1, waiting for transfers between devices, on_device(): lax.all_to_all(grad_slots, ('snd', 'mesh'), split_axis=0, concat_axis=0,...  42 us
    all_to_all x1, blocking collectives, on_device(): lax.all_to_all(requests, ('snd', 'mesh'), split_axis=0, concat_axis=0, ti...  36.1 us
    ppermute x3, starting transfers between devices, with_halo(): before = lax.ppermute(last, axis, up)  10 us
    all_to_all x1, starting transfers between devices, on_device(): lax.all_to_all(grad_slots, ('snd', 'mesh'), split_axis=0, concat_axis=0,...  9.04 us
    ppermute x3, waiting for transfers between devices, with_halo(): after = lax.ppermute(leading, axis, down)  8.34 us
    all_to_all x1, starting transfers between devices, on_device(): lax.all_to_all(looked, ('snd', 'mesh'), split_axis=0, concat_axis=0, tile...  5.47 us
  transfers between devices with their start and end apart: 9, of which 7 were waited for; matrix products, arithmetic and copies ran while one was open for 3% of the time, Pallas kernels for 0%

commit v1 on v0

v1 whole, which is shorter than its diff:
```python
import functools
import jax
import jax.numpy as jnp
from jax import lax
from jax.sharding import PartitionSpec as P
from jax.experimental import pallas as pl
from jax.experimental.pallas import tpu as pltpu

NZ = 48
ITERS = 4
ROWS = 8
BLOCKS = 192
LAYER = 24
HALO = ITERS - 1
EXT = ROWS + 2 * HALO
OWN0 = HALO * LAYER
HSZ = HALO * LAYER
ESZ = EXT * LAYER
N_OWN = 128
N_MESH = 4
N_FREQ = 4
PER = BLOCKS // N_FREQ
LOCAL = 64
F32 = jnp.float32
BF16 = jnp.bfloat16
I32 = jnp.int32
MESH = pl.DeviceIdType.MESH


def iota(shape, dim):
    return lax.broadcasted_iota(I32, shape, dim)


def onehot(mask):
    return jnp.where(mask, 1.0, 0.0).astype(BF16)


def pick(rows, values):
    high = values.astype(BF16)
    low = (values - high.astype(F32)).astype(BF16)
    dot = functools.partial(jnp.dot, preferred_element_type=F32)
    return dot(rows, high) + dot(rows, low)


def kernel(
    omegas, background, count, owner_in, local_in, cond, source_hbm, adjoint_hbm,
    field_hbm, grad_out,
    src_raw, adj_raw, src, adj, sig, fld, crl,
    ask, wanted, replies, fetched, shared, grads, summed, slots, arrived, partial_,
    in_sem, out_sem, ask_s, ask_r, rep_s, rep_r, sh_s, sh_r, hs_s, hs_r, hw_s, hw_r,
    rs_s, rs_r, gr_s, gr_r, ps_s, ps_r,
):
    s, f, m = lax.axis_index("snd"), lax.axis_index("freq"), lax.axis_index("mesh")
    z, core = s // 2, s % 2
    me = s * N_MESH + m

    def each_peer(act):
        def group(dz, with_self):
            for dm in (2, 1, 3, 0):
                for flip in (0, 1):
                    if with_self and dm == 0 and flip == 0:
                        continue
                    act(((z + dz) % 16) * 2 + (core if flip == 0 else 1 - core), (m + dm) % N_MESH)

        def body(i, carry):
            group(8 + (1 - 2 * (i % 2)) * ((i + 1) // 2), False)
            return carry

        lax.fori_loop(0, 15, body, 0)
        group(0, True)

    barrier = pltpu.get_barrier_semaphore()

    def greet(ps, pm):
        pl.semaphore_signal(barrier, inc=1, device_id={"snd": ps, "mesh": pm}, device_id_type=MESH)

    each_peer(greet)
    for k in range(1, N_FREQ):
        pl.semaphore_signal(
            barrier, inc=1, device_id={"freq": (f + k) % N_FREQ}, device_id_type=MESH
        )

    def remote(a, b, ss, rs, **to):
        return pltpu.make_async_remote_copy(
            src_ref=a, dst_ref=b, send_sem=ss, recv_sem=rs, device_id=to, device_id_type=MESH
        )

    def wait(ref, sem):
        pltpu.make_async_copy(ref, ref, sem).wait()

    load_src = pltpu.make_async_copy(source_hbm.at[0], src_raw, in_sem.at[0])
    load_adj = pltpu.make_async_copy(adjoint_hbm.at[0, 0], adj_raw, in_sem.at[1])
    load_src.start()
    load_adj.start()

    eye = iota((BLOCKS, BLOCKS), 0) == iota((BLOCKS, BLOCKS), 1)

    def to_col(row):
        return jnp.sum(jnp.where(eye, row, 0), axis=1, keepdims=True)

    owner_row = owner_in[...]
    owner_col = to_col(owner_row)
    local_col = to_col(local_in[...])
    key_row = owner_row * 256 + iota((1, BLOCKS), 1)
    key_col = owner_col * 256 + iota((BLOCKS, 1), 0)
    pos_row = jnp.sum(jnp.where(key_col < key_row, 1, 0), axis=0, keepdims=True)
    pos_col = jnp.sum(jnp.where(key_row < key_col, 1, 0), axis=1, keepdims=True)
    place_row = (pos_row % N_FREQ) * PER + pos_row // N_FREQ
    place_col = (pos_col % N_FREQ) * PER + pos_col // N_FREQ
    owners = iota((1, N_OWN), 1)
    mine = (owner_col == owners) & (pos_col % N_FREQ == f)
    ask[...] = jnp.sum(jnp.where(mine, local_col + 1, 0), axis=0, keepdims=True)

    def spread(raw, out, first):
        for c in range(6):
            for k in range(LAYER):
                out[c, pl.ds(first + k, ROWS, stride=LAYER), :] = raw[c, :, k * 128 : (k + 1) * 128]

    load_src.wait()
    spread(src_raw, src, OWN0)

    pl.semaphore_wait(barrier, N_OWN - 1 + N_FREQ - 1)

    wanted[pl.ds(me, 1), :] = ask[...]
    each_peer(
        lambda ps, pm: remote(
            ask, wanted.at[pl.ds(me, 1)], ask_s, ask_r, snd=ps, mesh=pm
        ).start()
    )

    up, down = (m + 1) % N_MESH, (m + 3) % N_MESH

    def trade_layers(ref, ss, rs):
        remote(
            ref.at[:, pl.ds(OWN0 + BLOCKS - HSZ, HSZ)], ref.at[:, pl.ds(0, HSZ)], ss.at[0], rs.at[0], mesh=up
        ).start()
        remote(
            ref.at[:, pl.ds(OWN0, HSZ)], ref.at[:, pl.ds(OWN0 + BLOCKS, HSZ)], ss.at[1], rs.at[1], mesh=down
        ).start()

    def layers_in(ref, rs):
        wait(ref.at[:, pl.ds(0, HSZ)], rs.at[0])
        wait(ref.at[:, pl.ds(OWN0 + BLOCKS, HSZ)], rs.at[1])

    def layers_out(ref, ss):
        wait(ref.at[:, pl.ds(OWN0 + BLOCKS - HSZ, HSZ)], ss.at[0])
        wait(ref.at[:, pl.ds(OWN0, HSZ)], ss.at[1])

    trade_layers(src, hs_s, hs_r)

    load_adj.wait()
    spread(adj_raw, adj, 0)

    less_row = jnp.sum(jnp.where(owner_col < owners, 1, 0), axis=0, keepdims=True)
    many_row = jnp.sum(jnp.where(owner_col == owners, 1, 0), axis=0, keepdims=True)
    owners_c = iota((N_OWN, 1), 0)
    less_col = jnp.sum(jnp.where(owner_row < owners_c, 1, 0), axis=1, keepdims=True)
    many_col = jnp.sum(jnp.where(owner_row == owners_c, 1, 0), axis=1, keepdims=True)
    at_col = iota((PER, 1), 0) * N_FREQ + f
    at_row = iota((1, PER), 1) * N_FREQ + f
    squeeze = onehot((at_col >= less_row) & (at_col < less_row + many_row))
    widen = onehot((at_row >= less_col) & (at_row < less_col + many_col))
    unsort = onehot(place_col == iota((1, BLOCKS), 1))
    resort = onehot(iota((BLOCKS, 1), 0) == place_row)

    wait(wanted.at[pl.ds(0, N_OWN - 1)], ask_r)
    asked = jnp.sum(
        jnp.where(iota((N_OWN, N_OWN), 1) == me, wanted[...], 0), axis=1, keepdims=True
    )
    asked_row = jnp.sum(
        jnp.where(iota((N_OWN, N_OWN), 0) == iota((N_OWN, N_OWN), 1), asked, 0), axis=0, keepdims=True
    )
    look = onehot(asked - 1 == iota((1, LOCAL), 1))
    answer = pick(look, cond[...])
    for c in range(3):
        replies[c] = answer[:, c * 128 : (c + 1) * 128]
    each_peer(
        lambda ps, pm: remote(
            replies.at[:, pl.ds(ps * N_MESH + pm, 1)], fetched.at[:, pl.ds(me, 1)], rep_s, rep_r,
            snd=ps, mesh=pm,
        ).start()
    )
    fetched[:, pl.ds(me, 1), :] = replies[:, pl.ds(me, 1), :]
    wait(fetched.at[:, pl.ds(0, N_OWN - 1)], rep_r)

    own_part = pl.ds(pl.multiple_of(f * PER, 8), PER)
    for c in range(3):
        shared[c, own_part, :] = pick(squeeze, fetched[c])
    for k in range(1, N_FREQ):
        remote(
            shared.at[:, own_part], shared.at[:, own_part], sh_s, sh_r, freq=(f + k) % N_FREQ
        ).start()
    wait(shared.at[:, pl.ds(0, BLOCKS - PER)], sh_r)

    live = m * BLOCKS + iota((BLOCKS, 1), 0) < count[0]
    for c in range(3):
        sig[c, pl.ds(OWN0, BLOCKS), :] = jnp.where(live, pick(unsort, shared[c]), background[c])
    trade_layers(sig, hw_s, hw_r)
    layers_in(src, hs_r)
    layers_in(sig, hw_r)

    omega = omegas[0]
    low_keep = jnp.where(m > 0, 1.0, 0.0)
    high_keep = jnp.where(m < N_MESH - 1, 1.0, 0.0)
    shape = (LAYER, 128)
    lane = iota(shape, 1)
    cell = iota(shape, 0) * 128 + lane
    third = cell % NZ

    def shifted(x, by, axis_roll, wrap, zero):
        r = pltpu.roll(x, by % 128, 1)
        r = jnp.where(wrap, pltpu.roll(r, axis_roll, 0), r)
        return jnp.where(zero, 0.0, r)

    def sy(x):
        return shifted(x, -NZ, LAYER - 1, lane >= 128 - NZ, cell >= LAYER * 128 - NZ)

    def sz(x):
        return shifted(x, -1, LAYER - 1, lane == 127, third == NZ - 1)

    def by(x):
        return shifted(x, NZ, 1, lane < NZ, cell < NZ)

    def bz(x):
        return shifted(x, 1, 1, lane == 0, third == 0)

    def at(i):
        return pl.ds(pl.multiple_of(i * LAYER, 8), LAYER)

    def keep_src(i):
        return jnp.where(i < HALO, low_keep, jnp.where(i >= HALO + ROWS, high_keep, 1.0))

    def relax(i, sr, si, er, ei, w):
        rr, ri = sr, si
        if er is not None:
            rr = rr + w * ei
            ri = ri - w * er
        scale = 0.5 / (16.0 + w * w)
        nr = scale * (4.0 * rr + w * ri)
        ni = scale * (4.0 * ri - w * rr)
        if er is not None:
            nr, ni = er + nr, ei + ni
        return nr, ni

    def first(i, carry):
        keep = keep_src(i)
        for c in range(3):
            w = omega * sig[c, at(i), :]
            nr, ni = relax(i, src[c, at(i), :] * keep, src[c + 3, at(i), :] * keep, None, None, w)
            fld[c, at(i), :] = nr
            fld[c + 3, at(i), :] = ni
        return carry

    lax.fori_loop(0, EXT, first, 0)

    for it in range(1, ITERS):
        lo, hi = it, EXT - it

        def curl(i, carry):
            keep = jnp.where(i < HALO, low_keep, 1.0)
            for p in (0, 3):
                ex, ey, ez = (fld[p + c, at(i), :] for c in range(3))
                ny, nz = fld[p + 1, at(i + 1), :], fld[p + 2, at(i + 1), :]
                crl[p, at(i), :] = ((sy(ez) - ez) - (sz(ey) - ey)) * keep
                crl[p + 1, at(i), :] = ((sz(ex) - ex) - (nz - ez)) * keep
                crl[p + 2, at(i), :] = ((ny - ey) - (sy(ex) - ex)) * keep
            return carry

        lax.fori_loop(lo - 1, hi, curl, 0)

        def update(i, carry):
            keep = jnp.where(i >= HALO + ROWS, high_keep, 1.0)
            ksrc = keep_src(i)
            image = []
            for p in (0, 3):
                hx, hy, hz = (crl[p + c, at(i), :] for c in range(3))
                py, pz = crl[p + 1, at(i - 1), :], crl[p + 2, at(i - 1), :]
                image.append((bz(hy) - hy) - (by(hz) - hz))
                image.append((pz - hz) - (bz(hx) - hx))
                image.append((by(hx) - hx) - (py - hy))
            for c in range(3):
                w = omega * sig[c, at(i), :]
                er, ei = fld[c, at(i), :], fld[c + 3, at(i), :]
                nr, ni = relax(
                    i,
                    src[c, at(i), :] * ksrc - image[c] * keep,
                    src[c + 3, at(i), :] * ksrc - image[c + 3] * keep,
                    er, ei, w,
                )
                fld[c, at(i), :] = nr
                fld[c + 3, at(i), :] = ni
            return carry

        lax.fori_loop(lo, hi, update, 0)

    own = pl.ds(OWN0, BLOCKS)
    for c in range(3):
        sens = omega * (adj[c] * fld[c + 3, own, :] - adj[c + 3] * fld[c, own, :])
        grads[c] = pick(resort, jnp.where(live, sens, 0.0))
    for k in range(1, N_FREQ):
        to = (f + k) % N_FREQ
        remote(
            grads.at[:, pl.ds(pl.multiple_of(to * PER, 8), PER)], summed.at[f], rs_s, rs_r, freq=to
        ).start()
    summed[f] = grads[:, own_part, :]

    for c in range(6):
        for k in range(LAYER):
            src_raw[c, :, k * 128 : (k + 1) * 128] = fld[c, pl.ds(OWN0 + k, ROWS, stride=LAYER), :]
    store = pltpu.make_async_copy(src_raw, field_hbm.at[0, 0], out_sem)
    store.start()

    wait(summed.at[pl.ds(0, N_FREQ - 1)], rs_r)
    for c in range(3):
        total = (summed[0, c] + summed[1, c]) + (summed[2, c] + summed[3, c])
        slots[c] = pick(widen, total)
    each_peer(
        lambda ps, pm: remote(
            slots.at[:, pl.ds(ps * N_MESH + pm, 1)], arrived.at[:, pl.ds(me, 1)], gr_s, gr_r,
            snd=ps, mesh=pm,
        ).start()
    )
    arrived[:, pl.ds(me, 1), :] = slots[:, pl.ds(me, 1), :]
    collect = onehot(asked_row - 1 == iota((LOCAL, 1), 0))
    wait(arrived.at[:, pl.ds(0, N_OWN - 1)], gr_r)
    for c in range(3):
        partial_[f, c] = pick(collect, arrived[c])
    for k in range(1, N_FREQ):
        remote(partial_.at[f], partial_.at[f], ps_s, ps_r, freq=(f + k) % N_FREQ).start()
    wait(partial_.at[pl.ds(0, N_FREQ - 1)], ps_r)
    for c in range(3):
        grad_out[:, c * 128 : (c + 1) * 128] = (partial_[0, c] + partial_[1, c]) + (
            partial_[2, c] + partial_[3, c]
        )

    wait(wanted.at[pl.ds(0, N_OWN - 1)], ask_s)
    wait(fetched.at[:, pl.ds(0, N_OWN - 1)], rep_s)
    wait(shared.at[:, pl.ds(0, BLOCKS - PER)], sh_s)
    layers_out(src, hs_s)
    layers_out(sig, hw_s)
    wait(summed.at[pl.ds(0, N_FREQ - 1)], rs_s)
    wait(arrived.at[:, pl.ds(0, N_OWN - 1)], gr_s)
    wait(partial_.at[pl.ds(0, N_FREQ - 1)], ps_s)
    store.wait()


def on_device(
    source, adjoint, omegas, background, conductivity, block_owner, block_local, block_count
):
    smem = pl.BlockSpec(memory_space=pltpu.SMEM)
    vmem = pl.BlockSpec(memory_space=pltpu.VMEM)
    hbm = pl.BlockSpec(memory_space=pl.ANY)
    buf = lambda *shape: pltpu.VMEM(shape, F32)
    dma = pltpu.SemaphoreType.DMA
    return pl.pallas_call(
        kernel,
        out_shape=(
            jax.ShapeDtypeStruct(adjoint.shape, F32),
            jax.ShapeDtypeStruct(conductivity.shape, F32),
        ),
        in_specs=[smem, smem, smem, vmem, vmem, vmem, hbm, hbm],
        out_specs=(hbm, vmem),
        scratch_shapes=[
            buf(6, ROWS, LAYER * 128),
            buf(6, ROWS, LAYER * 128),
            buf(6, ESZ, 128),
            buf(6, BLOCKS, 128),
            buf(3, ESZ, 128),
            buf(6, ESZ, 128),
            buf(6, ESZ, 128),
            pltpu.VMEM((1, N_OWN), I32),
            pltpu.VMEM((N_OWN, N_OWN), I32),
            buf(3, N_OWN, 128),
            buf(3, N_OWN, 128),
            buf(3, BLOCKS, 128),
            buf(3, BLOCKS, 128),
            buf(N_FREQ, 3, PER, 128),
            buf(3, N_OWN, 128),
            buf(3, N_OWN, 128),
            buf(N_FREQ, 3, LOCAL, 128),
            dma((2,)),
            dma,
        ]
        + [dma] * 6
        + [dma((2,))] * 4
        + [dma] * 6,
        compiler_params=pltpu.CompilerParams(
            collective_id=0, has_side_effects=True, vmem_limit_bytes=40 << 20
        ),
    )(
        omegas, background, block_count, block_owner.reshape(1, BLOCKS), block_local,
        conductivity, source, adjoint,
    )


def solution(mesh):
    return jax.shard_map(
        on_device,
        mesh=mesh,
        in_specs=(
            P("snd", None, "mesh", None),
            P("snd", "freq", None, "mesh", None),
            P("freq"),
            P(),
            P(("snd", "mesh"), None),
            P("snd", "mesh", None),
            P("snd", "mesh"),
            P("snd"),
        ),
        out_specs=(P("snd", "freq", None, "mesh", None), P(("snd", "mesh"), None)),
        check_vma=False,
    )
```

time: 259 us -> 88.5 us (0.34)
  waiting for transfers between devices: 138 us -> 0 us
  Pallas kernels: 0 us -> 81.1 us
  blocking collectives: 36.1 us -> 0 us
  starting transfers between devices: 28.4 us -> 0 us
  other arithmetic: 17.1 us -> 0 us
  local copies, waits for them, and re-layouts: 20.3 us -> 5.14 us
  between operations: 16 us -> 1.98 us
    all_to_all x2 -> x0, waiting for transfers between devices: 84.4 us -> none  [the longest x1 42.4 us: on_device(): lax.all_to_all(looked, ('snd', 'mesh'), split_axis=0, concat_axis=0, tile...]
    pallas_call x0 -> x1, Pallas kernels: none -> 81.1 us  [on_device(): pl.pallas_call(kernel, out_shape=(jax.ShapeDtypeStruct(adjoint.shape, F32...]
    psum x1 -> x0, waiting for transfers between devices: 45.1 us -> none  [on_device(): gradient = lax.psum(partial_value, 'freq')]
    all_to_all x1 -> x0, blocking collectives: 36.1 us -> none  [on_device(): lax.all_to_all(requests, ('snd', 'mesh'), split_axis=0, concat_axis=0, ti...]
    all_to_all x2 -> x0, starting transfers between devices: 14.5 us -> none  [the longest x1 9.04 us: on_device(): lax.all_to_all(grad_slots, ('snd', 'mesh'), split_axis=0, concat_axis=0,...]
    ppermute x6 -> x0, starting transfers between devices: 13.9 us -> none  [the longest x3 10 us: with_halo(): before = lax.ppermute(last, axis, up)]
    slice x21 -> x0, local copies, waits for them, and re-layouts: 9.41 us -> none  [the longest x8 4.26 us: relax_step(): resid_imag = forcing[3:] - applied[3:] - weights * field_real]
    ppermute x6 -> x0, waiting for transfers between devices: 8.42 us -> none  [the longest x3 8.34 us: with_halo(): after = lax.ppermute(leading, axis, down)]
  transfers between devices with their start and end apart: 9 -> 0, of which waited for: 7 -> 0; matrix products, arithmetic and copies ran while one was open for 3% -> 0% of each run, Pallas kernels for 0% -> 0%
where the time goes in v1:
time: 88.5 us; the launch traced here: 88.3 us
  Pallas kernels  81.1 us (92%)
  local copies, waits for them, and re-layouts  5.14 us (6%)
  between operations  1.98 us (2%)
    pallas_call x1, Pallas kernels, on_device(): pl.pallas_call(kernel, out_shape=(jax.ShapeDtypeStruct(adjoint.shape, F32...  81.1 us
    unnamed x14, local copies, waits for them, and re-layouts  5.14 us

profile of v1, /device:TPU:1, one launch (start us, length us, event | category | flops | bytes accessed | tf_op | source)
XLA Modules:
  0.0 88.3 jit_solution(12448443240355312638)
XLA Ops:
  1.3 0.0 copy-start.4
  1.9 0.0 copy-start.3
  2.0 0.0 copy-start.5
  2.0 0.0 copy-done.4
  2.0 0.7 copy-done.3
  2.6 0.0 copy-done.5
  2.6 0.0 copy-start
  2.6 1.1 %copy-done = f32[1,6,8,3072]{3,2,1,0:T(8,128)S(1)} copy-done((f32[1,6,8,3072]{3,2,1,0:T(8,128)S(1)}, f32[1,6,8,3072]{3,2,1,0:T(8,128)}, u32[]{:S(2)}) %copy-start) | copy-done | bytes 589848
  3.7 0.0 copy-start.1
  3.7 1.1 %copy-done.1 = f32[1,1,6,8,3072]{4,3,2,1,0:T(8,128)S(1)} copy-done((f32[1,1,6,8,3072]{4,3,2,1,0:T(8,128)S(1)}, f32[1,1,6,8,3072]{4,3,2,1,0:T(8,128)}, u32[]{:S(2)}) %copy-start.1) | copy-done | bytes 589848
  4.8 0.0 copy-start.2
  4.8 0.9 %copy-done.2 = f32[64,384]{1,0:T(8,128)S(1)} copy-done((f32[64,384]{1,0:T(8,128)S(1)}, f32[64,384]{1,0:T(8,128)}, u32[]{:S(2)}) %copy-start.2) | copy-done | bytes 98328
  5.7 81.1 %shard_map.95 = (f32[1,1,6,8,3072]{4,3,2,1,0:T(8,128)S(1)}, f32[64,384]{1,0:T(8,128)S(1)}) custom-call(f32[1]{0:T(128)S(6)} %copy.12.omegas, f32[3]{0:T(128)S(1)} %copy-done.5, s32[1]{0:T(128)S(6)} %copy.13.count, s32[1,192]{1,0:T(1,128)S(1)} %bitcast.1, s32[1,192]{1,0:T(1,128)S(1)} %copy-done.4, f32[64,384]{1,0:T(8,128)S(1)} %copy-done.2, ...), custom_call_target="tpu_custom_call" | custom-call | tf_op jit(solution)/shard_map/pallas_call | solution.py:355
  86.8 0.8 copy.14
  87.6 0.6 copy.15
Async XLA Ops:
  1.3 0.7 copy-start.4
  1.9 0.7 copy-start.3
  2.0 0.7 copy-start.5
  2.6 1.1 %copy-start = (f32[1,6,8,3072]{3,2,1,0:T(8,128)S(1)}, f32[1,6,8,3072]{3,2,1,0:T(8,128)}, u32[]{:S(2)}) copy-start(f32[1,6,8,3072]{3,2,1,0:T(8,128)} %source_hbm.1) | copy-start | bytes 1769476
  3.7 1.1 %copy-start.1 = (f32[1,1,6,8,3072]{4,3,2,1,0:T(8,128)S(1)}, f32[1,1,6,8,3072]{4,3,2,1,0:T(8,128)}, u32[]{:S(2)}) copy-start(f32[1,1,6,8,3072]{4,3,2,1,0:T(8,128)} %adjoint_hbm.1) | copy-start | bytes 1769476
  4.8 0.9 %copy-start.2 = (f32[64,384]{1,0:T(8,128)S(1)}, f32[64,384]{1,0:T(8,128)}, u32[]{:S(2)}) copy-start(f32[64,384]{1,0:T(8,128)} %cond.1) | copy-start | bytes 294916

commit v2 on v1

v2 whole, which is shorter than its diff:
```python
import functools
import jax
import jax.numpy as jnp
from jax import lax
from jax.sharding import PartitionSpec as P
from jax.experimental import pallas as pl
from jax.experimental.pallas import tpu as pltpu

NZ = 48
ITERS = 4
ROWS = 8
BLOCKS = 192
LAYER = 24
HALO = ITERS - 1
EXT = ROWS + 2 * HALO
OWN0 = HALO * LAYER
HSZ = HALO * LAYER
ESZ = EXT * LAYER
N_OWN = 128
N_MESH = 4
N_FREQ = 4
PER = BLOCKS // N_FREQ
LOCAL = 64
F32 = jnp.float32
BF16 = jnp.bfloat16
I32 = jnp.int32
MESH = pl.DeviceIdType.MESH
CHUNKS = ((0, 2), (2, 1))


def iota(shape, dim):
    return lax.broadcasted_iota(I32, shape, dim)


def onehot(mask):
    return jnp.where(mask, 1.0, 0.0).astype(BF16)


def pick(rows, values):
    high = values.astype(BF16)
    low = (values - high.astype(F32)).astype(BF16)
    dot = functools.partial(jnp.dot, preferred_element_type=F32)
    return dot(rows, high) + dot(rows, low)


def kernel(
    omegas_hbm, background_hbm, count_hbm, owner_hbm, local_hbm, cond_hbm, source_hbm, adjoint_hbm,
    field_hbm, grad_hbm,
    omegas, background, count, owner_in, local_in, cond, grad_out, src_raw, adj_raw, src, adj, sig, wgt, fld, crl,
    ask, wanted, replies, fetched, shared, grads, summed, slots, arrived, partial_,
    in_sem, out_sem, ask_s, ask_r, rep_s, rep_r, sh_s, sh_r, hs_s, hs_r, hw_s, hw_r,
    rs_s, rs_r, gr_s, gr_r, ps_s, ps_r,
):
    s, f, m = lax.axis_index("snd"), lax.axis_index("freq"), lax.axis_index("mesh")
    z, core = s // 2, s % 2
    me = s * N_MESH + m

    def each_peer(act):
        def group(dz, with_self):
            for dm in (2, 1, 3, 0):
                for flip in (0, 1):
                    if with_self and dm == 0 and flip == 0:
                        continue
                    act(((z + dz) % 16) * 2 + (core if flip == 0 else 1 - core), (m + dm) % N_MESH)

        def body(i, carry):
            group(8 + (1 - 2 * (i % 2)) * ((i + 1) // 2), False)
            return carry

        lax.fori_loop(0, 15, body, 0)
        group(0, True)

    barrier = pltpu.get_barrier_semaphore()

    def greet(ps, pm):
        pl.semaphore_signal(barrier, inc=1, device_id={"snd": ps, "mesh": pm}, device_id_type=MESH)

    each_peer(greet)
    for k in range(1, N_FREQ):
        pl.semaphore_signal(
            barrier, inc=1, device_id={"freq": (f + k) % N_FREQ}, device_id_type=MESH
        )

    def remote(a, b, ss, rs, **to):
        return pltpu.make_async_remote_copy(
            src_ref=a, dst_ref=b, send_sem=ss, recv_sem=rs, device_id=to, device_id_type=MESH
        )

    def wait(ref, sem):
        pltpu.make_async_copy(ref, ref, sem).wait()

    load_src = pltpu.make_async_copy(source_hbm.at[0], src_raw, in_sem.at[0])
    load_adj = pltpu.make_async_copy(adjoint_hbm.at[0, 0], adj_raw, in_sem.at[1])
    small = [
        pltpu.make_async_copy(a, b, in_sem.at[2 + i])
        for i, (a, b) in enumerate(
            (
                (owner_hbm, owner_in),
                (local_hbm, local_in),
                (cond_hbm, cond),
                (omegas_hbm, omegas),
                (background_hbm, background),
                (count_hbm, count),
            )
        )
    ]
    for copy in small:
        copy.start()
    load_src.start()
    load_adj.start()
    for copy in small:
        copy.wait()

    eye = iota((BLOCKS, BLOCKS), 0) == iota((BLOCKS, BLOCKS), 1)

    def to_col(row):
        return jnp.sum(jnp.where(eye, row, 0), axis=1, keepdims=True)

    owner_row = owner_in[...]
    owner_col = to_col(owner_row)
    local_col = to_col(local_in[...])
    key_row = owner_row * 256 + iota((1, BLOCKS), 1)
    key_col = owner_col * 256 + iota((BLOCKS, 1), 0)
    pos_row = jnp.sum(jnp.where(key_col < key_row, 1, 0), axis=0, keepdims=True)
    pos_col = jnp.sum(jnp.where(key_row < key_col, 1, 0), axis=1, keepdims=True)
    place_row = (pos_row % N_FREQ) * PER + pos_row // N_FREQ
    place_col = (pos_col % N_FREQ) * PER + pos_col // N_FREQ
    owners = iota((1, N_OWN), 1)
    mine = (owner_col == owners) & (pos_col % N_FREQ == f)
    ask[...] = jnp.sum(jnp.where(mine, local_col + 1, 0), axis=0, keepdims=True)

    def spread(raw, out, first):
        for c in range(6):
            for k in range(LAYER):
                out[c, pl.ds(first + k, ROWS, stride=LAYER), :] = raw[c, :, k * 128 : (k + 1) * 128]

    load_src.wait()
    spread(src_raw, src, OWN0)

    pl.semaphore_wait(barrier, N_OWN - 1 + N_FREQ - 1)

    wanted[pl.ds(me, 1), :] = ask[...]
    each_peer(
        lambda ps, pm: remote(
            ask, wanted.at[pl.ds(me, 1)], ask_s, ask_r, snd=ps, mesh=pm
        ).start()
    )

    up, down = (m + 1) % N_MESH, (m + 3) % N_MESH

    def trade_layers(ref, ss, rs, first, number):
        part = pl.ds(first, number)
        remote(
            ref.at[part, pl.ds(OWN0 + BLOCKS - HSZ, HSZ)], ref.at[part, pl.ds(0, HSZ)],
            ss.at[0], rs.at[0], mesh=up,
        ).start()
        remote(
            ref.at[part, pl.ds(OWN0, HSZ)], ref.at[part, pl.ds(OWN0 + BLOCKS, HSZ)],
            ss.at[1], rs.at[1], mesh=down,
        ).start()

    def layers_in(ref, rs, first, number):
        part = pl.ds(first, number)
        wait(ref.at[part, pl.ds(0, HSZ)], rs.at[0])
        wait(ref.at[part, pl.ds(OWN0 + BLOCKS, HSZ)], rs.at[1])

    def layers_out(ref, ss, first, number):
        part = pl.ds(first, number)
        wait(ref.at[part, pl.ds(OWN0 + BLOCKS - HSZ, HSZ)], ss.at[0])
        wait(ref.at[part, pl.ds(OWN0, HSZ)], ss.at[1])

    trade_layers(src, hs_s, hs_r, 0, 6)

    load_adj.wait()
    spread(adj_raw, adj, 0)

    less_row = jnp.sum(jnp.where(owner_col < owners, 1, 0), axis=0, keepdims=True)
    many_row = jnp.sum(jnp.where(owner_col == owners, 1, 0), axis=0, keepdims=True)
    owners_c = iota((N_OWN, 1), 0)
    less_col = jnp.sum(jnp.where(owner_row < owners_c, 1, 0), axis=1, keepdims=True)
    many_col = jnp.sum(jnp.where(owner_row == owners_c, 1, 0), axis=1, keepdims=True)
    at_col = iota((PER, 1), 0) * N_FREQ + f
    at_row = iota((1, PER), 1) * N_FREQ + f
    squeeze = onehot((at_col >= less_row) & (at_col < less_row + many_row))
    widen = onehot((at_row >= less_col) & (at_row < less_col + many_col))
    unsort = onehot(place_col == iota((1, BLOCKS), 1))
    resort = onehot(iota((BLOCKS, 1), 0) == place_row)

    low_keep = jnp.where(m > 0, 1.0, 0.0)
    high_keep = jnp.where(m < N_MESH - 1, 1.0, 0.0)
    layers_in(src, hs_r, 0, 6)
    for c in range(6):
        src[c, 0:OWN0, :] = src[c, 0:OWN0, :] * low_keep
        src[c, OWN0 + BLOCKS : ESZ, :] = src[c, OWN0 + BLOCKS : ESZ, :] * high_keep

    wait(wanted.at[pl.ds(0, N_OWN - 1)], ask_r)
    asked = jnp.sum(
        jnp.where(iota((N_OWN, N_OWN), 1) == me, wanted[...], 0), axis=1, keepdims=True
    )
    look = onehot(asked - 1 == iota((1, LOCAL), 1))

    def scatter_rows(a, b, ss, rs, first, number):
        part = pl.ds(first, number)
        each_peer(
            lambda ps, pm: remote(
                a.at[part, pl.ds(ps * N_MESH + pm, 1)], b.at[part, pl.ds(me, 1)], ss, rs,
                snd=ps, mesh=pm,
            ).start()
        )
        b[part, pl.ds(me, 1), :] = a[part, pl.ds(me, 1), :]

    for k, (first, number) in enumerate(CHUNKS):
        for c in range(first, first + number):
            replies[c] = pick(look, cond[:, c * 128 : (c + 1) * 128])
        scatter_rows(replies, fetched, rep_s.at[k], rep_r.at[k], first, number)
    asked_row = jnp.sum(
        jnp.where(iota((N_OWN, N_OWN), 0) == iota((N_OWN, N_OWN), 1), asked, 0), axis=0, keepdims=True
    )

    own_part = pl.ds(pl.multiple_of(f * PER, 8), PER)
    for k, (first, number) in enumerate(CHUNKS):
        part = pl.ds(first, number)
        wait(fetched.at[part, pl.ds(0, N_OWN - 1)], rep_r.at[k])
        for c in range(first, first + number):
            shared[c, own_part, :] = pick(squeeze, fetched[c])
        for to in range(1, N_FREQ):
            remote(
                shared.at[part, own_part], shared.at[part, own_part], sh_s.at[k], sh_r.at[k],
                freq=(f + to) % N_FREQ,
            ).start()

    live = m * BLOCKS + iota((BLOCKS, 1), 0) < count[0]
    for k, (first, number) in enumerate(CHUNKS):
        wait(shared.at[pl.ds(first, number), pl.ds(0, BLOCKS - PER)], sh_r.at[k])
        for c in range(first, first + number):
            sig[c, pl.ds(OWN0, BLOCKS), :] = jnp.where(live, pick(unsort, shared[c]), background[c])
        trade_layers(sig, hw_s.at[k], hw_r.at[k], first, number)

    omega = omegas[0]
    shape = (LAYER, 128)
    lane = iota(shape, 1)
    cell = iota(shape, 0) * 128 + lane
    third = cell % NZ
    y_last, z_last = cell >= LAYER * 128 - NZ, third == NZ - 1
    y_first, z_first = cell < NZ, third == 0

    def at(i, offset=0):
        start = i * LAYER
        return pl.ds(pl.multiple_of(start, 8) if offset == 0 else start + offset, LAYER)

    def sy(x, after):
        return jnp.where(y_last, 0.0, pltpu.roll(jnp.where(lane < NZ, after, x), 128 - NZ, 1))

    def sz(x, after):
        return jnp.where(z_last, 0.0, pltpu.roll(jnp.where(lane < 1, after, x), 127, 1))

    def by(x, before):
        return jnp.where(y_first, 0.0, pltpu.roll(jnp.where(lane >= 128 - NZ, before, x), NZ, 1))

    def bz(x, before):
        return jnp.where(z_first, 0.0, pltpu.roll(jnp.where(lane >= 127, before, x), 1, 1))

    def begin(i):
        for c in range(3):
            w = omega * sig[c, at(i), :]
            scale = 0.5 / (16.0 + w * w)
            real, imag = 4.0 * scale, w * scale
            sr, si = src[c, at(i), :], src[c + 3, at(i), :]
            wgt[c, at(i), :] = w
            wgt[c + 3, at(i), :] = real
            wgt[c + 6, at(i), :] = imag
            fld[c, at(i), :] = real * sr + imag * si
            fld[c + 3, at(i), :] = real * si - imag * sr

    def curl(i, keep=None):
        for p in (0, 3):
            ex, ey, ez = (fld[p + c, at(i), :] for c in range(3))
            ax, ay, az = (fld[p + c, at(i, 1), :] for c in range(3))
            ny, nz = fld[p + 1, at(i + 1), :], fld[p + 2, at(i + 1), :]
            hx = (sy(ez, az) - ez) - (sz(ey, ay) - ey)
            hy = (sz(ex, ax) - ex) - (nz - ez)
            hz = (ny - ey) - (sy(ex, ax) - ex)
            for c, h in enumerate((hx, hy, hz)):
                crl[p + c, at(i), :] = h if keep is None else h * keep

    def update(i, keep=None):
        image = []
        for p in (0, 3):
            hx, hy, hz = (crl[p + c, at(i), :] for c in range(3))
            bx, bhy, bhz = (crl[p + c, at(i, -1), :] for c in range(3))
            py, pz = crl[p + 1, at(i - 1), :], crl[p + 2, at(i - 1), :]
            image.append((bz(hy, bhy) - hy) - (by(hz, bhz) - hz))
            image.append((pz - hz) - (bz(hx, bx) - hx))
            image.append((by(hx, bx) - hx) - (py - hy))
        if keep is not None:
            image = [v * keep for v in image]
        for c in range(3):
            w, real, imag = (wgt[c + 3 * k, at(i), :] for k in range(3))
            er, ei = fld[c, at(i), :], fld[c + 3, at(i), :]
            rr = src[c, at(i), :] - image[c] + w * ei
            ri = src[c + 3, at(i), :] - image[c + 3] - w * er
            fld[c, at(i), :] = er + (real * rr + imag * ri)
            fld[c + 3, at(i), :] = ei + (real * ri - imag * rr)

    def loop(lo, hi, act):
        def body(i, carry):
            act(i)
            return carry

        lax.fori_loop(lo, hi, body, 0)

    top = HALO + ROWS
    loop(HALO, top, begin)
    for it in range(1, ITERS):
        loop(HALO + it - 1, top - it, curl)
        loop(HALO + it, top - it, update)

    for k, (first, number) in enumerate(CHUNKS):
        layers_in(sig, hw_r.at[k], first, number)

    def edge_begin(i):
        begin(i)
        begin(i + top)

    loop(0, HALO, edge_begin)
    for it in range(1, ITERS):

        def edge_curl(j):
            low = it - 1 + j
            curl(low, jnp.where(low < HALO, low_keep, 1.0))
            curl(top - it + j)

        def edge_update(j):
            high = top - it + j
            update(it + j)
            update(high, jnp.where(high >= top, high_keep, 1.0))

        loop(0, HALO, edge_curl)
        loop(0, HALO, edge_update)

    own = pl.ds(OWN0, BLOCKS)
    for k, (first, number) in enumerate(CHUNKS):
        part = pl.ds(first, number)
        for c in range(first, first + number):
            sens = omega * (adj[c] * fld[c + 3, own, :] - adj[c + 3] * fld[c, own, :])
            grads[c] = pick(resort, jnp.where(live, sens, 0.0))
        for to in range(1, N_FREQ):
            peer = (f + to) % N_FREQ
            remote(
                grads.at[part, pl.ds(pl.multiple_of(peer * PER, 8), PER)], summed.at[f, part],
                rs_s.at[k], rs_r.at[k], freq=peer,
            ).start()
        summed[f, part] = grads[part, own_part, :]

    collect = onehot(asked_row - 1 == iota((LOCAL, 1), 0))
    for k, (first, number) in enumerate(CHUNKS):
        wait(summed.at[pl.ds(0, N_FREQ - 1), pl.ds(first, number)], rs_r.at[k])
        for c in range(first, first + number):
            total = (summed[0, c] + summed[1, c]) + (summed[2, c] + summed[3, c])
            slots[c] = pick(widen, total)
        scatter_rows(slots, arrived, gr_s.at[k], gr_r.at[k], first, number)

    for c in range(6):
        for k in range(LAYER):
            src_raw[c, :, k * 128 : (k + 1) * 128] = fld[c, pl.ds(OWN0 + k, ROWS, stride=LAYER), :]
    store = pltpu.make_async_copy(src_raw, field_hbm.at[0, 0], out_sem.at[0])
    store.start()

    for k, (first, number) in enumerate(CHUNKS):
        part = pl.ds(first, number)
        wait(arrived.at[part, pl.ds(0, N_OWN - 1)], gr_r.at[k])
        for c in range(first, first + number):
            partial_[f, c] = pick(collect, arrived[c])
        for to in range(1, N_FREQ):
            remote(
                partial_.at[f, part], partial_.at[f, part], ps_s.at[k], ps_r.at[k],
                freq=(f + to) % N_FREQ,
            ).start()
    for k, (first, number) in enumerate(CHUNKS):
        wait(partial_.at[pl.ds(0, N_FREQ - 1), pl.ds(first, number)], ps_r.at[k])
        for c in range(first, first + number):
            grad_out[:, c * 128 : (c + 1) * 128] = (partial_[0, c] + partial_[1, c]) + (
                partial_[2, c] + partial_[3, c]
            )
    store_grad = pltpu.make_async_copy(grad_out, grad_hbm, out_sem.at[1])
    store_grad.start()

    wait(wanted.at[pl.ds(0, N_OWN - 1)], ask_s)
    layers_out(src, hs_s, 0, 6)
    for k, (first, number) in enumerate(CHUNKS):
        part = pl.ds(first, number)
        wait(fetched.at[part, pl.ds(0, N_OWN - 1)], rep_s.at[k])
        wait(shared.at[part, pl.ds(0, BLOCKS - PER)], sh_s.at[k])
        layers_out(sig, hw_s.at[k], first, number)
        wait(summed.at[pl.ds(0, N_FREQ - 1), part], rs_s.at[k])
        wait(arrived.at[part, pl.ds(0, N_OWN - 1)], gr_s.at[k])
        wait(partial_.at[pl.ds(0, N_FREQ - 1), part], ps_s.at[k])
    store.wait()
    store_grad.wait()


def settle(field, gradient, field_out, gradient_out, held, held_gradient, sem_in, sem_out):
    ways = [(field.at[0, 0, c], held.at[c], field_out.at[0, 0, c]) for c in range(6)]
    ways.append((gradient, held_gradient, gradient_out))
    loads = [pltpu.make_async_copy(a, b, sem_in.at[i]) for i, (a, b, _) in enumerate(ways)]
    stores = [pltpu.make_async_copy(b, c, sem_out.at[i]) for i, (_, b, c) in enumerate(ways)]
    for load in loads:
        load.start()
    for load, store in zip(loads, stores):
        load.wait()
        store.start()
    for store in stores:
        store.wait()


def on_device(
    source, adjoint, omegas, background, conductivity, block_owner, block_local, block_count
):
    hbm = pl.BlockSpec(memory_space=pltpu.HBM)
    buf = lambda *shape: pltpu.VMEM(shape, F32)
    dma = pltpu.SemaphoreType.DMA
    parts = len(CHUNKS)
    field, gradient = pl.pallas_call(
        kernel,
        out_shape=(
            jax.ShapeDtypeStruct(adjoint.shape, F32),
            jax.ShapeDtypeStruct(conductivity.shape, F32),
        ),
        in_specs=[hbm] * 8,
        out_specs=(hbm, hbm),
        scratch_shapes=[
            pltpu.SMEM((1,), F32),
            pltpu.SMEM((3,), F32),
            pltpu.SMEM((1,), I32),
            pltpu.VMEM((1, BLOCKS), I32),
            pltpu.VMEM((1, BLOCKS), I32),
            buf(LOCAL, 384),
            buf(LOCAL, 384),
            buf(6, ROWS, LAYER * 128),
            buf(6, ROWS, LAYER * 128),
            buf(6, ESZ, 128),
            buf(6, BLOCKS, 128),
            buf(3, ESZ, 128),
            buf(9, ESZ, 128),
            buf(6, ESZ, 128),
            buf(6, ESZ, 128),
            pltpu.VMEM((1, N_OWN), I32),
            pltpu.VMEM((N_OWN, N_OWN), I32),
            buf(3, N_OWN, 128),
            buf(3, N_OWN, 128),
            buf(3, BLOCKS, 128),
            buf(3, BLOCKS, 128),
            buf(N_FREQ, 3, PER, 128),
            buf(3, N_OWN, 128),
            buf(3, N_OWN, 128),
            buf(N_FREQ, 3, LOCAL, 128),
            dma((8,)),
            dma((2,)),
        ]
        + [dma] * 2
        + [dma((parts,))] * 4
        + [dma((2,))] * 2
        + [dma((parts, 2))] * 2
        + [dma((parts,))] * 6,
        compiler_params=pltpu.CompilerParams(
            collective_id=0, has_side_effects=True, vmem_limit_bytes=56 << 20
        ),
    )(
        omegas, background, block_count, block_owner.reshape(1, BLOCKS), block_local,
        conductivity, source, adjoint,
    )
    return pl.pallas_call(
        settle,
        out_shape=(
            jax.ShapeDtypeStruct(field.shape, F32),
            jax.ShapeDtypeStruct(gradient.shape, F32),
        ),
        in_specs=[hbm] * 2,
        out_specs=(hbm, hbm),
        scratch_shapes=[buf(6, ROWS, LAYER * 128), buf(LOCAL, 384), dma((7,)), dma((7,))],
        compiler_params=pltpu.CompilerParams(vmem_limit_bytes=56 << 20),
    )(field, gradient)


def solution(mesh):
    return jax.shard_map(
        on_device,
        mesh=mesh,
        in_specs=(
            P("snd", None, "mesh", None),
            P("snd", "freq", None, "mesh", None),
            P("freq"),
            P(),
            P(("snd", "mesh"), None),
            P("snd", "mesh", None),
            P("snd", "mesh"),
            P("snd"),
        ),
        out_specs=(P("snd", "freq", None, "mesh", None), P(("snd", "mesh"), None)),
        check_vma=False,
    )
```

time: 88.5 us -> 77.9 us (0.88)
  Pallas kernels: 81.1 us -> 75.8 us
  local copies, waits for them, and re-layouts: 5.14 us -> 0 us
    pallas_call x1, Pallas kernels: 81.1 us -> 73.8 us  [on_device(): pl.pallas_call(kernel, out_shape=(jax.ShapeDtypeStruct(adjoint.shape, F32...]
    unnamed x14 -> x0, local copies, waits for them, and re-layouts: 5.14 us -> none
    pallas_call x0 -> x1, Pallas kernels: none -> 1.94 us  [on_device(): pl.pallas_call(settle, out_shape=(jax.ShapeDtypeStruct(field.shape, F32),...]
where the time goes in v2:
time: 77.9 us; the launch traced here: 77.7 us
  Pallas kernels  75.8 us (97%)
  between operations  1.93 us (2%)
    pallas_call x1, Pallas kernels, on_device(): pl.pallas_call(kernel, out_shape=(jax.ShapeDtypeStruct(adjoint.shape, F32...  73.8 us
    pallas_call x1, Pallas kernels, on_device(): pl.pallas_call(settle, out_shape=(jax.ShapeDtypeStruct(field.shape, F32),...  1.94 us

profile of v2, /device:TPU:1, one launch (start us, length us, event | category | flops | bytes accessed | tf_op | source)
XLA Modules:
  0.0 77.7 jit_solution(10164785514954574589)
XLA Ops:
  1.9 73.8 %shard_map.95 = (f32[1,1,6,8,3072]{4,3,2,1,0:T(8,128)}, f32[64,384]{1,0:T(8,128)}) custom-call(f32[1]{0:T(128)S(6)} %copy.10.omegas_hbm, f32[3]{0:T(128)} %background_hbm.1, s32[1]{0:T(128)S(6)} %copy.11.count_hbm, s32[1,192]{1,0:T(1,128)} %bitcast.1, s32[1,192]{1,0:T(1,128)} %local_hbm.1, f32[64,384]{1,0:T(8,128)} %cond_hbm.1, ...), custom_call_target="tpu_custom_call" | custom-call | tf_op jit(solution)/shard_map/pallas_call | solution.py:423
  75.8 1.9 %shard_map.96 = (f32[1,1,6,8,3072]{4,3,2,1,0:T(8,128)}, f32[64,384]{1,0:T(8,128)}) custom-call(f32[1,1,6,8,3072]{4,3,2,1,0:T(8,128)} %get-tuple-element.4.field, f32[64,384]{1,0:T(8,128)} %get-tuple-element.5.gradient), custom_call_target="tpu_custom_call" | custom-call | tf_op jit(solution)/shard_map/pallas_call | solution.py:472

commit v3 on v2

--- a/solution.py
+++ b/solution.py
@@ -25,7 +25,8 @@
 BF16 = jnp.bfloat16
 I32 = jnp.int32
 MESH = pl.DeviceIdType.MESH
-CHUNKS = ((0, 2), (2, 1))
+FETCH = ((0, 2), (2, 1))
+SUMS = ((0, 2), (2, 1))
 
 
 def iota(shape, dim):
@@ -209,7 +210,7 @@
         )
         b[part, pl.ds(me, 1), :] = a[part, pl.ds(me, 1), :]
 
-    for k, (first, number) in enumerate(CHUNKS):
+    for k, (first, number) in enumerate(FETCH):
         for c in range(first, first + number):
             replies[c] = pick(look, cond[:, c * 128 : (c + 1) * 128])
         scatter_rows(replies, fetched, rep_s.at[k], rep_r.at[k], first, number)
@@ -218,7 +219,7 @@
     )
 
     own_part = pl.ds(pl.multiple_of(f * PER, 8), PER)
-    for k, (first, number) in enumerate(CHUNKS):
+    for k, (first, number) in enumerate(FETCH):
         part = pl.ds(first, number)
         wait(fetched.at[part, pl.ds(0, N_OWN - 1)], rep_r.at[k])
         for c in range(first, first + number):
@@ -230,7 +231,7 @@
             ).start()
 
     live = m * BLOCKS + iota((BLOCKS, 1), 0) < count[0]
-    for k, (first, number) in enumerate(CHUNKS):
+    for k, (first, number) in enumerate(FETCH):
         wait(shared.at[pl.ds(first, number), pl.ds(0, BLOCKS - PER)], sh_r.at[k])
         for c in range(first, first + number):
             sig[c, pl.ds(OWN0, BLOCKS), :] = jnp.where(live, pick(unsort, shared[c]), background[c])
@@ -315,14 +316,15 @@
         loop(HALO + it - 1, top - it, curl)
         loop(HALO + it, top - it, update)
 
-    for k, (first, number) in enumerate(CHUNKS):
+    for k, (first, number) in enumerate(FETCH):
         layers_in(sig, hw_r.at[k], first, number)
 
     def edge_begin(i):
         begin(i)
         begin(i + top)
 
-    loop(0, HALO, edge_begin)
+    for j in range(HALO):
+        edge_begin(j)
     for it in range(1, ITERS):
 
         def edge_curl(j):
@@ -335,11 +337,13 @@
             update(it + j)
             update(high, jnp.where(high >= top, high_keep, 1.0))
 
-        loop(0, HALO, edge_curl)
-        loop(0, HALO, edge_update)
+        for j in range(HALO):
+            edge_curl(j)
+        for j in range(HALO):
+            edge_update(j)
 
     own = pl.ds(OWN0, BLOCKS)
-    for k, (first, number) in enumerate(CHUNKS):
+    for k, (first, number) in enumerate(SUMS):
         part = pl.ds(first, number)
         for c in range(first, first + number):
             sens = omega * (adj[c] * fld[c + 3, own, :] - adj[c + 3] * fld[c, own, :])
@@ -353,7 +357,7 @@
         summed[f, part] = grads[part, own_part, :]
 
     collect = onehot(asked_row - 1 == iota((LOCAL, 1), 0))
-    for k, (first, number) in enumerate(CHUNKS):
+    for k, (first, number) in enumerate(SUMS):
         wait(summed.at[pl.ds(0, N_FREQ - 1), pl.ds(first, number)], rs_r.at[k])
         for c in range(first, first + number):
             total = (summed[0, c] + summed[1, c]) + (summed[2, c] + summed[3, c])
@@ -366,7 +370,7 @@
     store = pltpu.make_async_copy(src_raw, field_hbm.at[0, 0], out_sem.at[0])
     store.start()
 
-    for k, (first, number) in enumerate(CHUNKS):
+    for k, (first, number) in enumerate(SUMS):
         part = pl.ds(first, number)
         wait(arrived.at[part, pl.ds(0, N_OWN - 1)], gr_r.at[k])
         for c in range(first, first + number):
@@ -376,7 +380,7 @@
                 partial_.at[f, part], partial_.at[f, part], ps_s.at[k], ps_r.at[k],
                 freq=(f + to) % N_FREQ,
             ).start()
-    for k, (first, number) in enumerate(CHUNKS):
+    for k, (first, number) in enumerate(SUMS):
         wait(partial_.at[pl.ds(0, N_FREQ - 1), pl.ds(first, number)], ps_r.at[k])
         for c in range(first, first + number):
             grad_out[:, c * 128 : (c + 1) * 128] = (partial_[0, c] + partial_[1, c]) + (
@@ -387,11 +391,13 @@
 
     wait(wanted.at[pl.ds(0, N_OWN - 1)], ask_s)
     layers_out(src, hs_s, 0, 6)
-    for k, (first, number) in enumerate(CHUNKS):
+    for k, (first, number) in enumerate(FETCH):
         part = pl.ds(first, number)
         wait(fetched.at[part, pl.ds(0, N_OWN - 1)], rep_s.at[k])
         wait(shared.at[part, pl.ds(0, BLOCKS - PER)], sh_s.at[k])
         layers_out(sig, hw_s.at[k], first, number)
+    for k, (first, number) in enumerate(SUMS):
+        part = pl.ds(first, number)
         wait(summed.at[pl.ds(0, N_FREQ - 1), part], rs_s.at[k])
         wait(arrived.at[part, pl.ds(0, N_OWN - 1)], gr_s.at[k])
         wait(partial_.at[pl.ds(0, N_FREQ - 1), part], ps_s.at[k])
@@ -419,7 +425,6 @@
     hbm = pl.BlockSpec(memory_space=pltpu.HBM)
     buf = lambda *shape: pltpu.VMEM(shape, F32)
     dma = pltpu.SemaphoreType.DMA
-    parts = len(CHUNKS)
     field, gradient = pl.pallas_call(
         kernel,
         out_shape=(
@@ -458,10 +463,10 @@
             dma((2,)),
         ]
         + [dma] * 2
-        + [dma((parts,))] * 4
+        + [dma((len(FETCH),))] * 4
         + [dma((2,))] * 2
-        + [dma((parts, 2))] * 2
-        + [dma((parts,))] * 6,
+        + [dma((len(FETCH), 2))] * 2
+        + [dma((len(SUMS),))] * 6,
         compiler_params=pltpu.CompilerParams(
             collective_id=0, has_side_effects=True, vmem_limit_bytes=56 << 20
         ),

time: 77.9 us -> 76.6 us (0.983)
  Pallas kernels: 75.8 us -> 74.4 us
    pallas_call x1, Pallas kernels: 73.8 us -> 72.5 us  [on_device(): pl.pallas_call(kernel, out_shape=(jax.ShapeDtypeStruct(adjoint.shape, F32...]
where the time goes in v3:
time: 76.6 us; the launch traced here: 76.4 us
  Pallas kernels  74.4 us (97%)
  between operations  1.93 us (3%)
    pallas_call x1, Pallas kernels, on_device(): pl.pallas_call(kernel, out_shape=(jax.ShapeDtypeStruct(adjoint.shape, F32...  72.5 us
    pallas_call x1, Pallas kernels, on_device(): pl.pallas_call(settle, out_shape=(jax.ShapeDtypeStruct(field.shape, F32),...  1.94 us

profile of v3, /device:TPU:1, one launch (start us, length us, event | category | flops | bytes accessed | tf_op | source)
XLA Modules:
  0.0 76.4 jit_solution(2269465621287636841)
XLA Ops:
  1.9 72.5 %shard_map.95 = (f32[1,1,6,8,3072]{4,3,2,1,0:T(8,128)}, f32[64,384]{1,0:T(8,128)}) custom-call(f32[1]{0:T(128)S(6)} %copy.10.omegas_hbm, f32[3]{0:T(128)} %background_hbm.1, s32[1]{0:T(128)S(6)} %copy.11.count_hbm, s32[1,192]{1,0:T(1,128)} %bitcast.1, s32[1,192]{1,0:T(1,128)} %local_hbm.1, f32[64,384]{1,0:T(8,128)} %cond_hbm.1, ...), custom_call_target="tpu_custom_call" | custom-call | tf_op jit(solution)/shard_map/pallas_call | solution.py:428
  74.4 1.9 %shard_map.96 = (f32[1,1,6,8,3072]{4,3,2,1,0:T(8,128)}, f32[64,384]{1,0:T(8,128)}) custom-call(f32[1,1,6,8,3072]{4,3,2,1,0:T(8,128)} %get-tuple-element.4.field, f32[64,384]{1,0:T(8,128)} %get-tuple-element.5.gradient), custom_call_target="tpu_custom_call" | custom-call | tf_op jit(solution)/shard_map/pallas_call | solution.py:477

commit v4 on v3

--- a/solution.py
+++ b/solution.py
@@ -26,7 +26,7 @@
 I32 = jnp.int32
 MESH = pl.DeviceIdType.MESH
 FETCH = ((0, 2), (2, 1))
-SUMS = ((0, 2), (2, 1))
+SUMS = ((0, 1), (1, 1), (2, 1))
 
 
 def iota(shape, dim):

time: 76.6 us -> 76 us (level)
  no operation moved by 1% of the time
where the time goes in v4:
time: 76 us; the launch traced here: 75.8 us
  Pallas kernels  73.9 us (97%)
  between operations  1.93 us (3%)
    pallas_call x1, Pallas kernels, on_device(): pl.pallas_call(kernel, out_shape=(jax.ShapeDtypeStruct(adjoint.shape, F32...  71.9 us
    pallas_call x1, Pallas kernels, on_device(): pl.pallas_call(settle, out_shape=(jax.ShapeDtypeStruct(field.shape, F32),...  1.94 us

profile of v4, /device:TPU:1, one launch (start us, length us, event | category | flops | bytes accessed | tf_op | source)
XLA Modules:
  0.0 75.8 jit_solution(13721393609660921529)
XLA Ops:
  1.9 71.9 %shard_map.95 = (f32[1,1,6,8,3072]{4,3,2,1,0:T(8,128)}, f32[64,384]{1,0:T(8,128)}) custom-call(f32[1]{0:T(128)S(6)} %copy.10.omegas_hbm, f32[3]{0:T(128)} %background_hbm.1, s32[1]{0:T(128)S(6)} %copy.11.count_hbm, s32[1,192]{1,0:T(1,128)} %bitcast.1, s32[1,192]{1,0:T(1,128)} %local_hbm.1, f32[64,384]{1,0:T(8,128)} %cond_hbm.1, ...), custom_call_target="tpu_custom_call" | custom-call | tf_op jit(solution)/shard_map/pallas_call | solution.py:428
  73.9 1.9 %shard_map.96 = (f32[1,1,6,8,3072]{4,3,2,1,0:T(8,128)}, f32[64,384]{1,0:T(8,128)}) custom-call(f32[1,1,6,8,3072]{4,3,2,1,0:T(8,128)} %get-tuple-element.4.field, f32[64,384]{1,0:T(8,128)} %get-tuple-element.5.gradient), custom_call_target="tpu_custom_call" | custom-call | tf_op jit(solution)/shard_map/pallas_call | solution.py:477
